TPU v7x, 128 devices: a whole 4x4x4 slice. The times are simulated.
128 devices in a mesh: lat: 8 (over y_lo, x), lon: 16 (over y_hi, z, core).
Axes of the slice: x: 4, y: 4 (y_hi: 2, y_lo: 2; y = y_hi * 2 + y_lo), z: 4, core: 2. Of those that a mesh axis runs over, the one named last changes fastest.
Arguments:
- tokens: bfloat16 [4, 4, 48, 192, 512], P(None, None, 'lat', 'lon'), may hold values from -6 to 6
- norm1_gain: float32 [512], replicated, may hold values from 0.1 to 1.9
- qkv1: bfloat16 [512, 1536], replicated, may hold values from -1.5 to 1.5, as said below
- proj1: bfloat16 [512, 512], replicated, may hold values from -0.25 to 0.25
- norm2_gain: float32 [512], replicated, may hold values from 0.1 to 1.9
- mlp_in: bfloat16 [512, 2048], replicated, may hold values from -0.25 to 0.25
- mlp_out: bfloat16 [2048, 512], replicated, may hold values from -0.125 to 0.125
- merge_gain: float32 [2048], replicated, may hold values from 0.1 to 1.9
- merge_weight: bfloat16 [2048, 1024], replicated, may hold values from -0.125 to 0.125
- norm3_gain: float32 [1024], replicated, may hold values from 0.1 to 1.9
- qkv2: bfloat16 [1024, 3072], replicated, may hold values from -1.5 to 1.5, as said below
- proj2: bfloat16 [1024, 1024], replicated, may hold values from -0.1875 to 0.1875
Outputs:
- level1_out: bfloat16 [4, 4, 48, 192, 512], P(None, None, 'lat', 'lon')
- level2_out: bfloat16 [4, 4, 24, 96, 1024], P(None, None, 'lat')
Inputs may be any that keep to these rules, and one draw needn't show every extreme that they name: `qkv1`: columns hold the query, key and value projections in that order, heads contiguous. `qkv2`: columns hold the query, key and value projections in that order, heads contiguous.
All inputs are finite; a program needn't handle non-finite values.
Results may differ from a plain program's by a relative error of at most 0.015.
Values may be sent and summed in bfloat16 or wider, within the bound.
A program may use at most 256 MiB of HBM per device.

v0:
```python
import functools

import jax
import jax.numpy as jnp
import ml_dtypes
import numpy as np
from jax import lax
from jax.experimental import pallas as pl
from jax.experimental.pallas import tpu as pltpu
from jax.sharding import PartitionSpec as P

F32 = jnp.float32
BF16 = jnp.bfloat16
MESH = pl.DeviceIdType.MESH

MEMBERS, LEVELS, ROWS, COLS, D = 4, 4, 6, 12, 512
CELLS = LEVELS * ROWS * COLS
QUAD = CELLS // 4
SLAB = 40
LAT, LON = 8, 16
CROWS, CCOLS, D2 = 3, 6, 1024
HEADS2 = 16
HALF = 144


def quad_cells():
    cells = []
    for rh in range(2):
        for ch in range(2):
            for levels in ((1, 2), (0, 3)):
                for lev in levels:
                    for r in range(3):
                        for c in range(6):
                            cells.append((lev, rh * 3 + r, ch * 6 + c))
    return cells


def one_hot(rows, width):
    out = np.zeros((len(rows), width), ml_dtypes.bfloat16)
    for i, row in enumerate(rows):
        if row >= 0:
            out[i, row] = 1
    return out


def reorderings():
    cells = quad_cells()
    place = {cell: i for i, cell in enumerate(cells)}
    gather = one_hot([(r * COLS + c) * LEVELS + lev for lev, r, c in cells], CELLS)
    scatter = np.ascontiguousarray(gather.T)
    window_rows = [q * 72 + lp * 36 + i for lp in range(2) for q in range(4) for i in range(36)]
    to_window = one_hot(window_rows, CELLS)
    from_window = np.ascontiguousarray(to_window.T)
    coarse_cells = [(lev, a, b) for lev in range(2) for a in range(CROWS) for b in range(CCOLS)]
    merge = []
    for da in range(2):
        for db in range(2):
            for group in range(2):
                merge += [place[(2 * group + lev, 2 * a + da, 2 * b + db)] for lev, a, b in coarse_cells]
                merge += [-1] * (SLAB - len(coarse_cells))
    merge = one_hot(merge, CELLS)
    compact = one_hot([group * SLAB + i for group in range(2) for i in range(36)], 2 * SLAB)
    band = one_hot(
        [d * 72 + k * 6 + c for k in range(12) for d in range(4) for c in range(6)], CELLS
    )
    return gather, scatter, to_window, from_window, merge, compact, band


def dot(a, b):
    return jnp.dot(a, b, preferred_element_type=F32)


def dot_t(a, b):
    return lax.dot_general(a, b, (((1,), (1,)), ((), ())), preferred_element_type=F32)


def norm_rows(values):
    mean = jnp.mean(values, -1, keepdims=True)
    centred = values - mean
    spread = jnp.mean(centred * centred, -1, keepdims=True)
    return centred * lax.rsqrt(spread + 1e-05)


def gelu(v):
    return 0.5 * v * (1.0 + lax.erf(v * np.float32(2.0**-0.5)))


def stack_slabs(ref, m):
    return jnp.concatenate([ref[m, q].astype(F32) for q in range(4)], axis=0).astype(BF16)


def attend(q_ref, q_rows, k_rows, q_at, k_at, v_at, bias):
    rows = q_rows[1]
    qp = q_ref[pl.ds(*q_rows), q_at : q_at + 128]
    kp = q_ref[pl.ds(*k_rows), k_at : k_at + 128]
    vp = q_ref[pl.ds(*k_rows), v_at : v_at + 128]
    first = lax.broadcasted_iota(jnp.int32, (rows, 128), 1) < 64
    outs = []
    for head in range(2):
        keep = first if head == 0 else ~first
        qh = jnp.where(keep, qp, jnp.zeros_like(qp))
        scores = dot_t(qh, kp) * 0.125 + bias
        weights = jnp.exp(scores - jnp.max(scores, -1, keepdims=True))
        total = jnp.sum(weights, -1, keepdims=True)
        outs.append(dot(weights.astype(BF16), vp) / total)
    return jnp.where(first, outs[0], outs[1])


def body(
    tok, gain1, gain2, gain_m, gain3, gather, scatter, to_win, from_win, merge, compact, band,
    qkv1_h, proj1_h, in_h, out_h, mw_h, qkv2_h, proj2_h,
    l1, l2,
    qkv1, proj1, w_in, w_out, mw, qkv2, proj2,
    xs, nrm, win, qkv, att, bko, bki, mid, acc, coarse, ns, nw, qkv_b, o2, at2, g,
    bias1, bias2,
    w_sem, hs, hr, bs, br, cs, cr, as_, ar, gs, gr,
):
    lat, lon = lax.axis_index("lat"), lax.axis_index("lon")
    north, south = lax.rem(lat + LAT - 1, LAT), lax.rem(lat + 1, LAT)
    west, east = lax.rem(lon + LON - 1, LON), lax.rem(lon + 1, LON)
    core = lax.rem(lon, 2)
    z = lax.rem(lon // 2, 4)
    yh = lon // 8
    lon_y = lax.rem(lon + 8, LON)
    zp, zm = lax.rem(z + 1, 4), lax.rem(z + 3, 4)
    z_far = lax.rem(z + 2, 4)
    other = lon + 1 - 2 * core

    def at(y, zz):
        return y * 8 + zz * 2 + core

    lon_zp, lon_zm = at(yh, zp), at(yh, zm)
    group_lat, group_lon = lat - lax.rem(lat, 2), lon - core
    level_group = lax.rem(lat, 2)
    mine = 2 * level_group + core
    peers = []
    for k in range(1, 4):
        j = lax.rem(mine + k, 4)
        peers.append((j, (group_lat + j // 2, group_lon + lax.rem(j, 2))))

    to_nbr = [(north, west), (north, lon), (lat, west)]
    from_nbr = [(south, east), (south, lon), (lat, east)]

    loads = []
    wide = HEADS2 // 2 * 64
    for i, (src, dst) in enumerate(
        [(qkv1_h, qkv1), (proj1_h, proj1), (in_h, w_in), (out_h, w_out), (mw_h, mw)]
    ):
        loads.append(pltpu.make_async_copy(src, dst, w_sem.at[i]))
    for part in range(3):
        columns = pl.ds(pl.multiple_of(part * D2 + core * wide, wide), wide)
        loads.append(
            pltpu.make_async_copy(
                qkv2_h.at[:, columns], qkv2.at[:, pl.ds(part * wide, wide)], w_sem.at[5 + part]
            )
        )
    loads.append(pltpu.make_async_copy(proj2_h, proj2, w_sem.at[8]))
    loads[0].start()

    barrier = pltpu.get_barrier_semaphore()
    partners = to_nbr + from_nbr + [dev for _, dev in peers]
    partners += [(lat, lon_y), (lat, lon_zp), (lat, lon_zm)]
    for dev in partners:
        pl.semaphore_signal(barrier, inc=1, device_id=dev, device_id_type=MESH)

    def remote(src, dst, send, recv, dev):
        return pltpu.make_async_remote_copy(
            src_ref=src, dst_ref=dst, send_sem=send, recv_sem=recv, device_id=dev, device_id_type=MESH
        )

    def halo(m, q):
        return remote(nrm.at[m, q], win.at[m, q], hs.at[m, q], hr.at[m, q], to_nbr[q])

    def back(m, q):
        return remote(bko.at[m, q], bki.at[m, q], bs.at[m, q], br.at[m, q], from_nbr[q])

    def spread(m, k):
        j, dev = peers[k]
        return remote(ns.at[m, j // 2], nw.at[m, mine], cs.at[m, k], cr.at[m, mine], dev)

    def spread_arrival(m, k):
        j, dev = peers[k]
        return remote(nw.at[m, j], nw.at[m, j], cs.at[m, k], cr.at[m, j], dev)

    def result(m, k):
        j, dev = peers[k]
        return remote(o2.at[m, j], at2.at[m, mine], as_.at[m, k], ar.at[m, mine], dev)

    def result_arrival(m, k):
        j, dev = peers[k]
        return remote(o2.at[m, j], at2.at[m, j], as_.at[m, k], ar.at[m, j], dev)

    def block(m, slot, send, dev):
        return remote(g.at[m, slot], g.at[m, slot], gs.at[m, send], gr.at[m, slot], (lat, dev))

    def arrived(m, slot):
        block(m, slot, 0, lon_y).wait_recv()

    def blocks_of(shape, dim, size):
        return lax.broadcasted_iota(jnp.int32, shape, dim) // size

    shape = (HALF, HALF)
    south_q = blocks_of(shape, 0, 72) != blocks_of(shape, 1, 72)
    level_a = lax.rem(blocks_of(shape, 0, 18), 2) != lax.rem(blocks_of(shape, 1, 18), 2)
    edge = jnp.where(lat == LAT - 1, np.float32(-1e30), np.float32(0.0))
    rows_bias = jnp.where(south_q, edge, 0.0)
    bias1[0] = rows_bias
    bias1[1] = jnp.where(level_a, np.float32(-1e30), rows_bias)
    empty = lax.rem(lax.broadcasted_iota(jnp.int32, (1, 4 * SLAB), 1), SLAB) >= 36
    bias2[...] = jnp.where(empty, np.float32(-1e30), np.float32(0.0))

    pl.semaphore_wait(barrier, len(partners))

    def start_member(m, carry):
        x = dot(gather[...], tok[m].astype(F32).reshape(CELLS, D).astype(BF16))
        xs[m] = x.astype(BF16)
        normed = (norm_rows(x) * gain1[...])
        for q in range(3):
            nrm[m, q] = normed[q * QUAD : (q + 1) * QUAD].astype(BF16)
            halo(m, q).start()
        win[m, 3] = normed[3 * QUAD :].astype(BF16)
        return carry

    lax.fori_loop(0, MEMBERS, start_member, 0)
    for load in loads[1:]:
        load.start()

    def window_attention(m):
        for q in range(3):
            halo(m, q).wait_recv()
        cells = dot(to_win[...], stack_slabs(win, m)).astype(BF16)
        for part in range(3):
            columns = slice(part * D, (part + 1) * D)
            qkv[:, columns] = dot(cells, qkv1[:, columns]).astype(BF16)
        for lp in range(2):
            rows = (lp * HALF, HALF)
            for pair in range(4):
                columns = pair * 128
                att[lp * HALF : (lp + 1) * HALF, columns : columns + 128] = attend(
                    qkv, rows, rows, columns, D + columns, 2 * D + columns, bias1[lp]
                ).astype(BF16)
        tile = dot(from_win[...], att[...])
        for q in range(3):
            bko[m, q] = tile[q * QUAD : (q + 1) * QUAD].astype(BF16)
            back(m, q).start()
        bki[m, 3] = tile[3 * QUAD :].astype(BF16)

    def feed_forward(m):
        for q in range(3):
            back(m, q).wait_recv()
        mid[...] = xs[m].astype(F32) + dot(stack_slabs(bki, m), proj1[...])
        normed = (norm_rows(mid[...]) * gain2[...]).astype(BF16)
        for part in range(4):
            columns = slice(part * D, (part + 1) * D)
            hidden = gelu(dot(normed, w_in[:, columns])).astype(BF16)
            partial = dot(hidden, w_out[columns, :])
            if part == 0:
                acc[...] = mid[...] + partial
            else:
                acc[...] += partial
        level1 = acc[...].astype(BF16)
        l1[m] = dot(scatter[...], level1).reshape(ROWS, COLS, LEVELS, D).astype(BF16)
        quarters = dot(merge[...], level1)
        parts = [quarters[k * 2 * SLAB : (k + 1) * 2 * SLAB] for k in range(4)]
        mean = sum(jnp.sum(p, -1, keepdims=True) for p in parts) * (1.0 / (4 * D))
        parts = [p - mean for p in parts]
        var = sum(jnp.sum(p * p, -1, keepdims=True) for p in parts) * (1.0 / (4 * D))
        scale = lax.rsqrt(var + 1e-05)
        merged = jnp.concatenate(
            [(p * scale * gain_m[:, k * D : (k + 1) * D]).astype(BF16) for k, p in enumerate(parts)],
            axis=1,
        )
        small = dot(merged, mw[...]).astype(BF16).astype(F32)
        coarse[m] = small
        normed3 = norm_rows(small) * gain3[...]
        for group in range(2):
            ns[m, group] = normed3[group * SLAB : (group + 1) * SLAB].astype(BF16)
        for k in range(3):
            spread(m, k).start()
        nw[m, mine] = ns[m, level_group]

    def heads_of_group(m):
        for k in range(3):
            spread_arrival(m, k).wait_recv()
        cells = stack_slabs(nw, m)
        for part in range(3):
            columns = slice(part * wide, (part + 1) * wide)
            qkv_b[:, columns] = dot(cells, qkv2[:, columns]).astype(BF16)
        rows = (0, 4 * SLAB)
        for pair in range(4):
            columns = pair * 128
            out = attend(qkv_b, rows, rows, columns, wide + columns, 2 * wide + columns, bias2[...])
            for d in range(4):
                o2[m, d, :, columns : columns + 128] = out[d * SLAB : (d + 1) * SLAB].astype(BF16)
        for k in range(3):
            result(m, k).start()
        at2[m, mine] = o2[m, mine]

    def project_out(m):
        for k in range(3):
            result_arrival(m, k).wait_recv()
        attended = jnp.concatenate(
            [
                jnp.concatenate([at2[m, 2 * group + half].astype(F32) for group in range(2)], axis=0)
                for half in range(2)
            ],
            axis=1,
        ).astype(BF16)
        level2 = (coarse[m] + dot(attended, proj2[...])).astype(BF16)
        g[m, lon] = dot(compact[...], level2).astype(BF16)
        block(m, lon, 0, lon_y).start()
        block(m, lon, 1, lon_zp).start()
        block(m, lon, 2, lon_zm).start()
        block(m, lon, 3, other).start()

    def after_y(m):
        arrived(m, lon_y)
        block(m, lon_y, 4, lon_zp).start()
        block(m, lon_y, 5, lon_zm).start()
        block(m, lon_y, 6, other).start()

    toward = 1 - 2 * core
    z_from = lax.rem(z + 4 - toward, 4)
    z_to = lax.rem(z + 4 + toward, 4)

    def after_z(m):
        for y in range(2):
            arrived(m, at(y, z_from))
            block(m, at(y, z_from), 7 + y, at(yh, z_to)).start()
            block(m, at(y, z_from), 9 + y, other).start()
        for y in range(2):
            arrived(m, at(y, z_to))
            block(m, at(y, z_to), 11 + y, other).start()

    def after_z2(m):
        for y in range(2):
            arrived(m, at(y, z_far))
            block(m, at(y, z_far), 13 + y, other).start()

    def lay_out(m):
        for y in range(2):
            for zz in range(4):
                arrived(m, y * 8 + zz * 2 + 1 - core)

        for half in range(2):
            pieces = []
            for quarter in range(2):
                first = half * 8 + quarter * 4
                slabs = jnp.concatenate([g[m, first + d].astype(F32) for d in range(4)], axis=0)
                pieces.append(dot(band[...], slabs.astype(BF16)).reshape(12, 24, D2))
            columns = jnp.concatenate(pieces, axis=1).astype(BF16)
            l2[m, :, :, half * 48 : (half + 1) * 48, :] = columns.reshape(LEVELS, CROWS, 48, D2)

    def when(t, lo, hi, phase, lag):
        @pl.when((t >= lo) & (t < hi))
        def _():
            phase(t - lag)

    def step(t, carry):
        @pl.when(t == 0)
        def _():
            loads[0].wait()

        when(t, 0, 4, window_attention, 0)

        @pl.when(t == 2)
        def _():
            for i in range(1, 5):
                loads[i].wait()

        when(t, 2, 6, feed_forward, 2)

        @pl.when(t == 3)
        def _():
            for i in range(5, 9):
                loads[i].wait()

        when(t, 4, 8, project_out, 4)
        when(t, 5, 9, after_z, 5)
        when(t, 3, 7, heads_of_group, 3)
        when(t, 4, 8, after_y, 4)
        when(t, 5, 9, after_z2, 5)
        when(t, 6, 10, lay_out, 6)
        return carry

    lax.fori_loop(0, 10, step, 0)

    def finish(m, carry):
        for q in range(3):
            halo(m, q).wait_send()
            back(m, q).wait_send()
            spread(m, q).wait_send()
            result(m, q).wait_send()
        for i in range(15):
            block(m, lon, i, lon_y).wait_send()
        return carry

    lax.fori_loop(0, MEMBERS, finish, 0)


def hand_out(l1_in, l2_in, l1, l2, sems):
    copies = [pltpu.make_async_copy(l2_in.at[m], l2.at[m], sems.at[m]) for m in range(MEMBERS)]
    copies.append(pltpu.make_async_copy(l1_in, l1, sems.at[MEMBERS]))
    for copy in copies:
        copy.start()
    for copy in copies:
        copy.wait()


def shards(
    tokens, norm1_gain, qkv1, proj1, norm2_gain, mlp_in, mlp_out, merge_gain, merge_weight,
    norm3_gain, qkv2, proj2,
):
    vmem = pl.BlockSpec(memory_space=pltpu.VMEM)
    hbm = pl.BlockSpec(memory_space=pl.ANY)
    dma = pltpu.SemaphoreType.DMA
    wide = HEADS2 // 2 * 64

    def bf(*dims):
        return pltpu.VMEM(dims, BF16)

    def fl(*dims):
        return pltpu.VMEM(dims, F32)

    level1, level2 = pl.pallas_call(
        body,
        name="encoder",
        out_shape=(
            pltpu.VMEM((MEMBERS, ROWS, COLS, LEVELS, D), BF16),
            pltpu.VMEM((MEMBERS, LEVELS, CROWS, LON * CCOLS, D2), BF16),
        ),
        in_specs=[vmem] * 12 + [hbm] * 7,
        out_specs=(vmem, vmem),
        scratch_shapes=[
            bf(D, 3 * D), bf(D, D), bf(D, 4 * D), bf(4 * D, D), bf(4 * D, D2), bf(D2, 3 * wide),
            bf(D2, D2),
            bf(MEMBERS, CELLS, D),
            bf(MEMBERS, 3, QUAD, D), bf(MEMBERS, 4, QUAD, D),
            bf(CELLS, 3 * D), bf(CELLS, D),
            bf(MEMBERS, 3, QUAD, D), bf(MEMBERS, 4, QUAD, D),
            fl(CELLS, D), fl(CELLS, D),
            fl(MEMBERS, 2 * SLAB, D2), bf(MEMBERS, 2, SLAB, D2), bf(MEMBERS, 4, SLAB, D2),
            bf(4 * SLAB, 3 * wide),
            bf(MEMBERS, 4, SLAB, wide), bf(MEMBERS, 4, SLAB, wide),
            bf(MEMBERS, LON, QUAD, D2),
            fl(2, HALF, HALF), fl(1, 4 * SLAB),
            dma((9,)),
            dma((MEMBERS, 3)), dma((MEMBERS, 3)),
            dma((MEMBERS, 3)), dma((MEMBERS, 3)),
            dma((MEMBERS, 3)), dma((MEMBERS, 4)),
            dma((MEMBERS, 3)), dma((MEMBERS, 4)),
            dma((MEMBERS, 15)), dma((MEMBERS, LON)),
        ],
        compiler_params=pltpu.CompilerParams(
            collective_id=0, has_side_effects=True, vmem_limit_bytes=48 * 2**20
        ),
        cost_estimate=pl.CostEstimate(flops=12 * 10**9, bytes_accessed=30 * 10**6, transcendentals=4 * 10**6),
    )(
        jnp.transpose(tokens, (0, 2, 3, 1, 4)), norm1_gain.reshape(1, D), norm2_gain.reshape(1, D), merge_gain.reshape(1, 4 * D),
        norm3_gain.reshape(1, D2), *[jnp.asarray(order) for order in reorderings()],
        qkv1, proj1, mlp_in, mlp_out, merge_weight, qkv2, proj2,
    )
    level1, level2 = pl.pallas_call(
        hand_out,
        name="hand_out",
        out_shape=(
            jax.ShapeDtypeStruct(level1.shape, BF16),
            jax.ShapeDtypeStruct(level2.shape, BF16),
        ),
        in_specs=[vmem, vmem],
        out_specs=(hbm, hbm),
        scratch_shapes=[dma((MEMBERS + 1,))],
        compiler_params=pltpu.CompilerParams(vmem_limit_bytes=2**20),
    )(level1, level2)
    return jnp.transpose(level1, (0, 3, 1, 2, 4)), level2


def solution(mesh):
    in_specs = (P(None, None, "lat", "lon", None),) + (P(),) * 11
    out_specs = (P(None, None, "lat", "lon", None), P(None, None, "lat", None, None))
    return jax.shard_map(shards, mesh=mesh, in_specs=in_specs, out_specs=out_specs, check_vma=False)
```

profile of v0, /device:TPU:20, one launch (start us, length us, event | category | flops | bytes accessed | tf_op | source)
XLA Modules:
  0.0 104.9 jit_solution(9611755333229630442)
XLA Ops:
  0.6 100.2 %encoder.1 = (bf16[4,6,12,4,512]{4,3,2,1,0:T(4,128)(2,1)S(1)}, bf16[4,4,3,96,1024]{4,3,2,1,0:T(8,128)(2,1)S(1)}) custom-call(bf16[4,6,12,4,512]{4,3,2,1,0:T(4,128)(2,1)} %bitcast.6, f32[1,512]{1,0:T(1,128)} %bitcast.10, f32[1,512]{1,0:T(1,128)} %bitcast.11, f32[1,2048]{1,0:T(1,128)} %bitcast.8, f32[1,1024]{1,0:T(1,128)} %bitcast.9, ...), custom_call_target="tpu_custom_call" | custom-call | flops 12000000000 | bytes 30000000 | tf_op jit(solution)/shard_map/encoder/pallas_call | solution.py:425
  100.8 4.0 %hand_out.1 = (bf16[4,6,12,4,512]{4,3,2,1,0:T(4,128)(2,1)}, bf16[4,4,3,96,1024]{4,3,2,1,0:T(8,128)(2,1)}) custom-call(bf16[4,6,12,4,512]{4,3,2,1,0:T(4,128)(2,1)S(1)} %get-tuple-element.6.l1_in, bf16[4,4,3,96,1024]{4,3,2,1,0:T(8,128)(2,1)S(1)} %get-tuple-element.7.l2_in), custom_call_target="tpu_custom_call" | custom-call | tf_op jit(solution)/shard_map/hand_out/pallas_call | solution.py:463
where the time goes:
time: 105 us
  Pallas kernels  104 us (99%)
    pallas_call x1, Pallas kernels, shards(): pl.pallas_call(body, name='encoder', out_shape=(pltpu.VMEM((MEMBERS, ROWS...  100 us
    pallas_call x1, Pallas kernels, shards(): pl.pallas_call(hand_out, name='hand_out', out_shape=(jax.ShapeDtypeStruct...  4.03 us

commit v1 on v0

--- a/solution.py
+++ b/solution.py
@@ -141,6 +141,13 @@
     to_nbr = [(north, west), (north, lon), (lat, west)]
     from_nbr = [(south, east), (south, lon), (lat, east)]
 
+    def one_way(m, here, there):
+        odd = lax.rem(m, 2)
+        return tuple(a + odd * (b - a) for a, b in zip(here, there))
+
+    def quadrant(m, k):
+        return k + lax.rem(m, 2) * (3 - 2 * k)
+
     loads = []
     wide = HEADS2 // 2 * 64
     for i, (src, dst) in enumerate(
@@ -168,11 +175,15 @@
             src_ref=src, dst_ref=dst, send_sem=send, recv_sem=recv, device_id=dev, device_id_type=MESH
         )
 
-    def halo(m, q):
-        return remote(nrm.at[m, q], win.at[m, q], hs.at[m, q], hr.at[m, q], to_nbr[q])
-
-    def back(m, q):
-        return remote(bko.at[m, q], bki.at[m, q], bs.at[m, q], br.at[m, q], from_nbr[q])
+    def halo(m, k):
+        dev = one_way(m, to_nbr[k], from_nbr[k])
+        q = quadrant(m, k)
+        return remote(nrm.at[m, q], win.at[m, q], hs.at[m, k], hr.at[m, k], dev)
+
+    def back(m, k):
+        dev = one_way(m, from_nbr[k], to_nbr[k])
+        q = quadrant(m, k)
+        return remote(bko.at[m, q], bki.at[m, q], bs.at[m, k], br.at[m, k], dev)
 
     def spread(m, k):
         j, dev = peers[k]
@@ -202,32 +213,44 @@
     shape = (HALF, HALF)
     south_q = blocks_of(shape, 0, 72) != blocks_of(shape, 1, 72)
     level_a = lax.rem(blocks_of(shape, 0, 18), 2) != lax.rem(blocks_of(shape, 1, 18), 2)
-    edge = jnp.where(lat == LAT - 1, np.float32(-1e30), np.float32(0.0))
-    rows_bias = jnp.where(south_q, edge, 0.0)
-    bias1[0] = rows_bias
-    bias1[1] = jnp.where(level_a, np.float32(-1e30), rows_bias)
+    for odd, last in ((0, LAT - 1), (1, 0)):
+        edge = jnp.where(lat == last, np.float32(-1e30), np.float32(0.0))
+        rows_bias = jnp.where(south_q, edge, 0.0)
+        bias1[odd, 0] = rows_bias
+        bias1[odd, 1] = jnp.where(level_a, np.float32(-1e30), rows_bias)
     empty = lax.rem(lax.broadcasted_iota(jnp.int32, (1, 4 * SLAB), 1), SLAB) >= 36
     bias2[...] = jnp.where(empty, np.float32(-1e30), np.float32(0.0))
 
-    pl.semaphore_wait(barrier, len(partners))
-
-    def start_member(m, carry):
+    def norm_member(m, carry):
         x = dot(gather[...], tok[m].astype(F32).reshape(CELLS, D).astype(BF16))
         xs[m] = x.astype(BF16)
         normed = (norm_rows(x) * gain1[...])
-        for q in range(3):
+        for q in range(4):
             nrm[m, q] = normed[q * QUAD : (q + 1) * QUAD].astype(BF16)
-            halo(m, q).start()
-        win[m, 3] = normed[3 * QUAD :].astype(BF16)
+        own = quadrant(m, 3)
+        win[m, own] = nrm[m, own]
         return carry
 
-    lax.fori_loop(0, MEMBERS, start_member, 0)
+    def send_halo(m):
+        for k in range(3):
+            halo(m, k).start()
+
+    lax.fori_loop(0, 2, norm_member, 0)
+    pl.semaphore_wait(barrier, len(partners))
+    send_halo(0)
+    send_halo(1)
     for load in loads[1:]:
         load.start()
+    lax.fori_loop(2, MEMBERS, norm_member, 0)
 
     def window_attention(m):
-        for q in range(3):
-            halo(m, q).wait_recv()
+        for k in range(3):
+            halo(m, k).wait_recv()
+
+        @pl.when(m < 2)
+        def _():
+            send_halo(m + 2)
+
         cells = dot(to_win[...], stack_slabs(win, m)).astype(BF16)
         for part in range(3):
             columns = slice(part * D, (part + 1) * D)
@@ -237,20 +260,28 @@
             for pair in range(4):
                 columns = pair * 128
                 att[lp * HALF : (lp + 1) * HALF, columns : columns + 128] = attend(
-                    qkv, rows, rows, columns, D + columns, 2 * D + columns, bias1[lp]
+                    qkv, rows, rows, columns, D + columns, 2 * D + columns, bias1[lax.rem(m, 2), lp]
                 ).astype(BF16)
         tile = dot(from_win[...], att[...])
-        for q in range(3):
+        for q in range(4):
             bko[m, q] = tile[q * QUAD : (q + 1) * QUAD].astype(BF16)
-            back(m, q).start()
-        bki[m, 3] = tile[3 * QUAD :].astype(BF16)
+        for k in range(3):
+            back(m, k).start()
+        own = quadrant(m, 3)
+        bki[m, own] = bko[m, own]
 
     def feed_forward(m):
-        for q in range(3):
-            back(m, q).wait_recv()
+        for k in range(3):
+            back(m, k).wait_recv()
         mid[...] = xs[m].astype(F32) + dot(stack_slabs(bki, m), proj1[...])
         normed = (norm_rows(mid[...]) * gain2[...]).astype(BF16)
         for part in range(4):
+            if part == 2:
+
+                @pl.when(m == 3)
+                def _():
+                    after_y(0)
+
             columns = slice(part * D, (part + 1) * D)
             hidden = gelu(dot(normed, w_in[:, columns])).astype(BF16)
             partial = dot(hidden, w_out[columns, :])
@@ -375,15 +406,29 @@
             for i in range(5, 9):
                 loads[i].wait()
 
-        when(t, 4, 8, project_out, 4)
-        when(t, 5, 9, after_z, 5)
-        when(t, 3, 7, heads_of_group, 3)
-        when(t, 4, 8, after_y, 4)
-        when(t, 5, 9, after_z2, 5)
-        when(t, 6, 10, lay_out, 6)
+        when(t, 4, 6, project_out, 4)
+        when(t, 3, 6, heads_of_group, 3)
         return carry
 
-    lax.fori_loop(0, 10, step, 0)
+    lax.fori_loop(0, 6, step, 0)
+    heads_of_group(3)
+    project_out(2)
+    after_z(0)
+    after_y(1)
+    project_out(3)
+    after_y(2)
+    after_z(1)
+    after_z2(0)
+    after_y(3)
+    after_z(2)
+    after_z2(1)
+    lay_out(0)
+    after_z(3)
+    after_z2(2)
+    lay_out(1)
+    after_z2(3)
+    lay_out(2)
+    lay_out(3)
 
     def finish(m, carry):
         for q in range(3):
@@ -399,8 +444,12 @@
 
 
 def hand_out(l1_in, l2_in, l1, l2, sems):
-    copies = [pltpu.make_async_copy(l2_in.at[m], l2.at[m], sems.at[m]) for m in range(MEMBERS)]
-    copies.append(pltpu.make_async_copy(l1_in, l1, sems.at[MEMBERS]))
+    copies = []
+    for i in range(MEMBERS * LEVELS):
+        m, lev = i // LEVELS, i % LEVELS
+        copies.append(pltpu.make_async_copy(l2_in.at[m, lev], l2.at[m, lev], sems.at[i]))
+    for m in range(MEMBERS):
+        copies.append(pltpu.make_async_copy(l1_in.at[m], l1.at[m], sems.at[MEMBERS * LEVELS + m]))
     for copy in copies:
         copy.start()
     for copy in copies:
@@ -435,15 +484,15 @@
             bf(D, 3 * D), bf(D, D), bf(D, 4 * D), bf(4 * D, D), bf(4 * D, D2), bf(D2, 3 * wide),
             bf(D2, D2),
             bf(MEMBERS, CELLS, D),
-            bf(MEMBERS, 3, QUAD, D), bf(MEMBERS, 4, QUAD, D),
+            bf(MEMBERS, 4, QUAD, D), bf(MEMBERS, 4, QUAD, D),
             bf(CELLS, 3 * D), bf(CELLS, D),
-            bf(MEMBERS, 3, QUAD, D), bf(MEMBERS, 4, QUAD, D),
+            bf(MEMBERS, 4, QUAD, D), bf(MEMBERS, 4, QUAD, D),
             fl(CELLS, D), fl(CELLS, D),
             fl(MEMBERS, 2 * SLAB, D2), bf(MEMBERS, 2, SLAB, D2), bf(MEMBERS, 4, SLAB, D2),
             bf(4 * SLAB, 3 * wide),
             bf(MEMBERS, 4, SLAB, wide), bf(MEMBERS, 4, SLAB, wide),
             bf(MEMBERS, LON, QUAD, D2),
-            fl(2, HALF, HALF), fl(1, 4 * SLAB),
+            fl(2, 2, HALF, HALF), fl(1, 4 * SLAB),
             dma((9,)),
             dma((MEMBERS, 3)), dma((MEMBERS, 3)),
             dma((MEMBERS, 3)), dma((MEMBERS, 3)),
@@ -469,7 +518,7 @@
         ),
         in_specs=[vmem, vmem],
         out_specs=(hbm, hbm),
-        scratch_shapes=[dma((MEMBERS + 1,))],
+        scratch_shapes=[dma((MEMBERS * (LEVELS + 1),))],
         compiler_params=pltpu.CompilerParams(vmem_limit_bytes=2**20),
     )(level1, level2)
     return jnp.transpose(level1, (0, 3, 1, 2, 4)), level2

time: 105 us -> 100 us (0.952)
  the two profiles are of different devices: /device:TPU:20 before, /device:TPU:1 now
where the time goes in v1:
time: 100 us; the launch traced here: 99.8 us
  Pallas kernels  99 us (99%)
    pallas_call x1, Pallas kernels, shards(): pl.pallas_call(body, name='encoder', out_shape=(pltpu.VMEM((MEMBERS, ROWS...  94.9 us
    pallas_call x1, Pallas kernels, shards(): pl.pallas_call(hand_out, name='hand_out', out_shape=(jax.ShapeDtypeStruct...  4.13 us

profile of v1, /device:TPU:1, one launch (start us, length us, event | category | flops | bytes accessed | tf_op | source)
XLA Modules:
  0.0 99.8 jit_solution(6241466502267336375)
XLA Ops:
  0.6 94.9 %encoder.1 = (bf16[4,6,12,4,512]{4,3,2,1,0:T(4,128)(2,1)S(1)}, bf16[4,4,3,96,1024]{4,3,2,1,0:T(8,128)(2,1)S(1)}) custom-call(bf16[4,6,12,4,512]{4,3,2,1,0:T(4,128)(2,1)} %bitcast.6, f32[1,512]{1,0:T(1,128)} %bitcast.10, f32[1,512]{1,0:T(1,128)} %bitcast.11, f32[1,2048]{1,0:T(1,128)} %bitcast.8, f32[1,1024]{1,0:T(1,128)} %bitcast.9, ...), custom_call_target="tpu_custom_call" | custom-call | flops 12000000000 | bytes 30000000 | tf_op jit(solution)/shard_map/encoder/pallas_call | solution.py:474
  95.5 4.1 %hand_out.1 = (bf16[4,6,12,4,512]{4,3,2,1,0:T(4,128)(2,1)}, bf16[4,4,3,96,1024]{4,3,2,1,0:T(8,128)(2,1)}) custom-call(bf16[4,6,12,4,512]{4,3,2,1,0:T(4,128)(2,1)S(1)} %get-tuple-element.6.l1_in, bf16[4,4,3,96,1024]{4,3,2,1,0:T(8,128)(2,1)S(1)} %get-tuple-element.7.l2_in), custom_call_target="tpu_custom_call" | custom-call | tf_op jit(solution)/shard_map/hand_out/pallas_call | solution.py:512

commit v2 on v1

--- a/solution.py
+++ b/solution.py
@@ -185,13 +185,24 @@
         q = quadrant(m, k)
         return remote(bko.at[m, q], bki.at[m, q], bs.at[m, k], br.at[m, k], dev)
 
+    across = 2 * (1 - level_group) + core
+    diagonal = across + 1 - 2 * core
+    beside = 2 * level_group + 1 - core
+    to_across, to_beside = (group_lat + 1 - level_group, lon), (lat, other)
+
     def spread(m, k):
-        j, dev = peers[k]
-        return remote(ns.at[m, j // 2], nw.at[m, mine], cs.at[m, k], cr.at[m, mine], dev)
+        src = (ns.at[m, 1 - level_group], ns.at[m, level_group], nw.at[m, across])[k]
+        slot = (mine, mine, across)[k]
+        dev = (to_across, to_beside, to_beside)[k]
+        return remote(src, nw.at[m, slot], cs.at[m, k], cr.at[m, slot], dev)
 
     def spread_arrival(m, k):
-        j, dev = peers[k]
-        return remote(nw.at[m, j], nw.at[m, j], cs.at[m, k], cr.at[m, j], dev)
+        j = (across, beside, diagonal)[k]
+        return remote(nw.at[m, j], nw.at[m, j], cs.at[m, k], cr.at[m, j], to_beside)
+
+    def pass_on(m):
+        spread_arrival(m, 0).wait_recv()
+        spread(m, 2).start()
 
     def result(m, k):
         j, dev = peers[k]
@@ -276,6 +287,12 @@
         mid[...] = xs[m].astype(F32) + dot(stack_slabs(bki, m), proj1[...])
         normed = (norm_rows(mid[...]) * gain2[...]).astype(BF16)
         for part in range(4):
+            if part == 2:
+
+                @pl.when(m >= 1)
+                def _():
+                    pass_on(m - 1)
+
             if part == 2:
 
                 @pl.when(m == 3)
@@ -306,12 +323,12 @@
         normed3 = norm_rows(small) * gain3[...]
         for group in range(2):
             ns[m, group] = normed3[group * SLAB : (group + 1) * SLAB].astype(BF16)
-        for k in range(3):
+        for k in range(2):
             spread(m, k).start()
         nw[m, mine] = ns[m, level_group]
 
     def heads_of_group(m):
-        for k in range(3):
+        for k in range(1, 3):
             spread_arrival(m, k).wait_recv()
         cells = stack_slabs(nw, m)
         for part in range(3):
@@ -411,9 +428,10 @@
         return carry
 
     lax.fori_loop(0, 6, step, 0)
+    pass_on(3)
+    after_z(0)
+    project_out(2)
     heads_of_group(3)
-    project_out(2)
-    after_z(0)
     after_y(1)
     project_out(3)
     after_y(2)

time: 100 us -> 95.5 us (0.955)
  Pallas kernels: 99 us -> 94.6 us
    pallas_call x1, Pallas kernels: 94.9 us -> 90.4 us  [shards(): pl.pallas_call(body, name='encoder', out_shape=(pltpu.VMEM((MEMBERS, ROWS...]
where the time goes in v2:
time: 95.5 us; the launch traced here: 95.4 us
  Pallas kernels  94.6 us (99%)
    pallas_call x1, Pallas kernels, shards(): pl.pallas_call(body, name='encoder', out_shape=(pltpu.VMEM((MEMBERS, ROWS...  90.4 us
    pallas_call x1, Pallas kernels, shards(): pl.pallas_call(hand_out, name='hand_out', out_shape=(jax.ShapeDtypeStruct...  4.13 us

profile of v2, /device:TPU:1, one launch (start us, length us, event | category | flops | bytes accessed | tf_op | source)
XLA Modules:
  0.0 95.4 jit_solution(18301370667617637205)
XLA Ops:
  0.6 90.4 %encoder.1 = (bf16[4,6,12,4,512]{4,3,2,1,0:T(4,128)(2,1)S(1)}, bf16[4,4,3,96,1024]{4,3,2,1,0:T(8,128)(2,1)S(1)}) custom-call(bf16[4,6,12,4,512]{4,3,2,1,0:T(4,128)(2,1)} %bitcast.6, f32[1,512]{1,0:T(1,128)} %bitcast.10, f32[1,512]{1,0:T(1,128)} %bitcast.11, f32[1,2048]{1,0:T(1,128)} %bitcast.8, f32[1,1024]{1,0:T(1,128)} %bitcast.9, ...), custom_call_target="tpu_custom_call" | custom-call | flops 12000000000 | bytes 30000000 | tf_op jit(solution)/shard_map/encoder/pallas_call | solution.py:492
  91.1 4.1 %hand_out.1 = (bf16[4,6,12,4,512]{4,3,2,1,0:T(4,128)(2,1)}, bf16[4,4,3,96,1024]{4,3,2,1,0:T(8,128)(2,1)}) custom-call(bf16[4,6,12,4,512]{4,3,2,1,0:T(4,128)(2,1)S(1)} %get-tuple-element.6.l1_in, bf16[4,4,3,96,1024]{4,3,2,1,0:T(8,128)(2,1)S(1)} %get-tuple-element.7.l2_in), custom_call_target="tpu_custom_call" | custom-call | tf_op jit(solution)/shard_map/hand_out/pallas_call | solution.py:530

commit v3 on v2

--- a/solution.py
+++ b/solution.py
@@ -431,8 +431,8 @@
     pass_on(3)
     after_z(0)
     project_out(2)
+    after_y(1)
     heads_of_group(3)
-    after_y(1)
     project_out(3)
     after_y(2)
     after_z(1)

time: 95.5 us -> 95.5 us (level)
  no operation moved by 1% of the time
where the time goes in v3:
time: 95.5 us; the launch traced here: 95.4 us
  Pallas kernels  94.6 us (99%)
    pallas_call x1, Pallas kernels, shards(): pl.pallas_call(body, name='encoder', out_shape=(pltpu.VMEM((MEMBERS, ROWS...  90.4 us
    pallas_call x1, Pallas kernels, shards(): pl.pallas_call(hand_out, name='hand_out', out_shape=(jax.ShapeDtypeStruct...  4.13 us

profile of v3, /device:TPU:1, one launch (start us, length us, event | category | flops | bytes accessed | tf_op | source)
XLA Modules:
  0.0 95.4 jit_solution(16564997708851380323)
XLA Ops:
  0.6 90.4 %encoder.1 = (bf16[4,6,12,4,512]{4,3,2,1,0:T(4,128)(2,1)S(1)}, bf16[4,4,3,96,1024]{4,3,2,1,0:T(8,128)(2,1)S(1)}) custom-call(bf16[4,6,12,4,512]{4,3,2,1,0:T(4,128)(2,1)} %bitcast.6, f32[1,512]{1,0:T(1,128)} %bitcast.10, f32[1,512]{1,0:T(1,128)} %bitcast.11, f32[1,2048]{1,0:T(1,128)} %bitcast.8, f32[1,1024]{1,0:T(1,128)} %bitcast.9, ...), custom_call_target="tpu_custom_call" | custom-call | flops 12000000000 | bytes 30000000 | tf_op jit(solution)/shard_map/encoder/pallas_call | solution.py:492
  91.1 4.1 %hand_out.1 = (bf16[4,6,12,4,512]{4,3,2,1,0:T(4,128)(2,1)}, bf16[4,4,3,96,1024]{4,3,2,1,0:T(8,128)(2,1)}) custom-call(bf16[4,6,12,4,512]{4,3,2,1,0:T(4,128)(2,1)S(1)} %get-tuple-element.6.l1_in, bf16[4,4,3,96,1024]{4,3,2,1,0:T(8,128)(2,1)S(1)} %get-tuple-element.7.l2_in), custom_call_target="tpu_custom_call" | custom-call | tf_op jit(solution)/shard_map/hand_out/pallas_call | solution.py:530
